TPU v7x, 128 devices: a whole 4x4x4 slice. The times are simulated.
128 devices in a mesh: leaf: 8 (over y, core), front: 16 (over x, z).
Axes of the slice: x: 4, y: 4, z: 4, core: 2. Of those that a mesh axis runs over, the one named last changes fastest.
Arguments:
- inv_factors: bfloat16 [8, 2, 1024, 1024], P('leaf', None, 'front')
- panel_rows: bfloat16 [8, 1024, 1024], P('leaf', 'front'), may hold values from -6 to 6
- border: bfloat16 [8, 2048, 2048], P('leaf', 'front'), may hold values from -6 to 6
- tail: bfloat16 [8, 2048, 2048], P('leaf', 'front'), may hold values from -6 to 6
- front_sizes: int32 [8], replicated, may hold values from 1024 to 2048, as said below
- block_map: int32 [8, 16], replicated, may hold values from 0 to 31, as said below
- block_owner: int32 [8, 32], replicated, may hold values from 0 to 47, as said below
Outputs:
- link_factor: bfloat16 [8, 1024, 1024], P('leaf', 'front')
- border_factor: bfloat16 [8, 2048, 2048], P('leaf', 'front')
- parent_update: float32 [8, 4096, 6144], P('leaf', None, 'front')
Inputs may be any that keep to these rules, and one draw needn't show every extreme that they name: `front_sizes`: the live rows of some child always equal 2048; every child has at least 1024. `block_map`: the entries of one child's row are distinct. `block_owner`: the entries of one parent's row are distinct; slot s belongs to front index s // 3, so no front index owns more than 3 blocks of a parent, and in every parent's row one front index owns exactly 3.
All inputs are finite; a program needn't handle non-finite values.
Results may differ from a plain program's by a relative error of at most 0.0055.
Values may be sent and summed in bfloat16 or wider, within the bound.
No kernel may reach another device: no remote copies, remote signals or barrier semaphores. Data moves between devices by JAX's collectives and lax.ppermute only.
A program may use at most 64 MiB of HBM per device.

v0:
```python
import jax
import jax.numpy as jnp
from jax import lax
from jax.sharding import PartitionSpec as P

PANEL = 1024
BLOCK = 128
SLOTS = 3


def passed_along(value, axis, by):
    devices = lax.axis_size(axis)
    return lax.ppermute(value, axis, [(i, (i + by) % devices) for i in range(devices)])


def dot_rows(left_rows, right_rows):
    return lax.dot_general(
        left_rows, right_rows, (((1,), (1,)), ((), ())), preferred_element_type=jnp.float32
    )


def against(left_rows, piece):
    return dot_rows(left_rows, piece)


def pick_row(table, index):
    chooser = (jnp.arange(table.shape[0], dtype=jnp.int32)[:, None] == index).astype(jnp.int32)
    return jnp.sum(chooser * table, axis=0)


def route_tiles(contribution, owner_line, child_map, nfront, parent_blocks):
    block_pick = (child_map[:, None] == jnp.arange(parent_blocks, dtype=jnp.int32)[None, :]).astype(
        jnp.int32
    )
    slot_index = jnp.sum(block_pick * owner_line[None, :], axis=1)
    owner_front = slot_index // SLOTS
    owner_slot = slot_index % SLOTS
    select = (jnp.arange(nfront, dtype=jnp.int32)[:, None, None] == owner_front[None, None, :]) & (
        jnp.arange(SLOTS, dtype=jnp.int32)[None, :, None] == owner_slot[None, None, :]
    )
    tiles = contribution.reshape(BLOCK, nfront, BLOCK)
    return jnp.einsum(
        "ocb,rbd->orcd", select.astype(jnp.bfloat16), tiles, preferred_element_type=jnp.float32
    ).astype(jnp.bfloat16)


def place_rows(arrived, child_map, nfront, parent_blocks):
    row_hot = (jnp.arange(parent_blocks, dtype=jnp.int32)[:, None] == child_map[None, :]).astype(
        jnp.bfloat16
    )
    merged = jnp.dot(
        row_hot, arrived.reshape(nfront, BLOCK * SLOTS * BLOCK), preferred_element_type=jnp.float32
    )
    return merged.reshape(parent_blocks * BLOCK, SLOTS * BLOCK)


def per_device(inv_factors, panel_rows, border, tail, front_sizes, block_map, block_owner):
    nfront = lax.axis_size("front")
    nleaf = lax.axis_size("leaf")
    half_leaf = nleaf // 2
    leaf_group = lax.axis_index("leaf")
    front_place = lax.axis_index("front")
    first_inv = inv_factors[0, 0]
    second_inv = inv_factors[0, 1]
    upper_rows = panel_rows[0]
    left_cols = border[0, :, :PANEL]
    right_cols = border[0, :, PANEL:]
    stacked = jnp.concatenate([upper_rows, left_cols], axis=0)
    upper_count = upper_rows.shape[0]
    projected = against(stacked, lax.all_gather(first_inv, "front", axis=0, tiled=True))
    projected = projected.astype(jnp.bfloat16)
    link_local = projected[:upper_count]
    first_local = projected[upper_count:]
    coupled = against(first_local, lax.all_gather(link_local, "front", axis=0, tiled=True))
    updated = (right_cols.astype(jnp.float32) - coupled).astype(jnp.bfloat16)
    second_local = against(updated, lax.all_gather(second_inv, "front", axis=0, tiled=True))
    second_local = second_local.astype(jnp.bfloat16)
    factor_local = jnp.concatenate([first_local, second_local], axis=1)
    schur = tail[0].astype(jnp.float32) - against(
        factor_local, lax.all_gather(factor_local, "front", axis=0, tiled=True)
    )
    contrib_rows = BLOCK * nfront
    live = front_sizes[leaf_group]
    row_global = front_place * BLOCK + jnp.arange(BLOCK, dtype=jnp.int32)
    col_global = jnp.arange(contrib_rows, dtype=jnp.int32)
    keep = (row_global[:, None] < live) & (col_global[None, :] < live)
    contribution = jnp.where(keep, schur, jnp.float32(0.0)).astype(jnp.bfloat16)
    parent_blocks = 2 * nfront
    parent_group = (leaf_group + half_leaf) % nleaf
    child_group = (leaf_group + nleaf - half_leaf) % nleaf
    child_map_here = pick_row(block_map, child_group)
    own_map = pick_row(block_map, leaf_group)
    routed = route_tiles(
        contribution, pick_row(block_owner, parent_group), own_map, nfront, parent_blocks
    )
    sorted_tiles = lax.all_to_all(routed, "front", split_axis=0, concat_axis=0, tiled=True)
    arrived = passed_along(sorted_tiles, "leaf", half_leaf)
    merged = place_rows(arrived, child_map_here, nfront, parent_blocks)
    return (link_local[None], factor_local[None], merged[None])


def solution(mesh):
    return jax.shard_map(
        per_device,
        mesh=mesh,
        in_specs=(
            P("leaf", None, "front", None),
            P("leaf", "front", None),
            P("leaf", "front", None),
            P("leaf", "front", None),
            P(),
            P(),
            P(),
        ),
        out_specs=(P("leaf", "front", None), P("leaf", "front", None), P("leaf", None, "front")),
        check_vma=False,
    )
```

profile of v0, /device:TPU:0, one launch (start us, length us, event | category | flops | bytes accessed | tf_op | source)
XLA Modules:
  0.0 320.9 jit_solution(9470419997501196426)
XLA Ops:
  7.2 1.7 fusion.33
  9.0 0.7 all-gather.13.cloned.1.call-update
  9.7 1.0 slice_bitcast_fusion
  10.7 47.8 %all-gather.11.cloned.1.call-done = bf16[1,1,1024,1024]{3,2,1,0:T(8,128)(2,1)} async-done(((bf16[1,1,64,1024]{3,2,1,0:T(8,128)(2,1)}), bf16[1,1,1024,1024]{3,2,1,0:T(8,128)(2,1)}) %all-gather.11.cloned.1.call-update) | async-done | bytes 2097168 | tf_op jit(solution)/shard_map/all_gather | solution.py:70
  58.5 2.5 fusion.7
  61.0 0.7 fusion.32
  61.8 43.9 %all-gather.13.cloned.1.call-done = bf16[1,1,1024,1024]{3,2,1,0:T(8,128)(2,1)} async-done(((bf16[1,1,64,1024]{3,2,1,0:T(8,128)(2,1)}), bf16[1,1,1024,1024]{3,2,1,0:T(8,128)(2,1)}) %all-gather.13.cloned.1.call-update) | async-done | bytes 2097168 | tf_op jit(solution)/shard_map/all_gather | solution.py:76
  105.7 47.3 %all-gather.7.cloned.1.call-done = bf16[1024,1024]{1,0:T(8,128)(2,1)} async-done(((bf16[64,1024]{1,0:T(8,128)(2,1)}), bf16[1024,1024]{1,0:T(8,128)(2,1)}) %all-gather.7.cloned.1.call-update) | async-done | bytes 2097168 | tf_op jit(solution)/shard_map/all_gather | solution.py:74
  153.0 3.7 %fusion.11 = bf16[128,1024]{1,0:T(8,128)(2,1)S(1)} fusion(bf16[1,1,1024,1024]{3,2,1,0:T(8,128)(2,1)} %all-gather.13.cloned.1.call-done, bf16[1024,1024]{1,0:T(8,128)(2,1)} %all-gather.7.cloned.1.call-done, bf16[1,128,2048]{2,1,0:T(8,128)(2,1)S(1)} %copy-done.1, bf16[192,1024]{1,0:T(8,128)(2,1)S(1)} %fusion.7), kind=kOutput, calls=%fused_computation.12 | convolution fusion | flops 537395200 | bytes 4980736 | tf_op jit(solution)/shard_map/dot_general | solution.py:17
  156.8 1.1 pad_maximum_fusion
  158.0 0.7 dynamic_slice.3
  158.6 0.7 add_compare_fusion
  159.3 0.7 iota_compare_fusion.4
  160.5 67.8 %all-gather.9.cloned.1.call-done = bf16[2048,2048]{1,0:T(8,128)(2,1)} async-done(((bf16[128,2048]{1,0:T(8,128)(2,1)}), bf16[2048,2048]{1,0:T(8,128)(2,1)}) %all-gather.9.cloned.1.call-update) | async-done | bytes 8388624 | tf_op jit(solution)/shard_map/all_gather | solution.py:80
  228.2 6.3 %fusion.10 = bf16[16,8,16,128]{3,1,2,0:T(8,128)(2,1)S(1)} fusion(bf16[2048,2048]{1,0:T(8,128)(2,1)} %all-gather.9.cloned.1.call-done, bf16[1,128,2048]{2,1,0:T(8,128)(2,1)S(1)} %copy-done, pred[2048]{0:T(1024)(128)(4,1)S(1)} %iota_compare_fusion.4, pred[128]{0:T(512)(128)(4,1)S(1)} %add_compare_fusion, bf16[128,1024]{1,0:T(8,128)(2,1)S(1)} %fusion.11, ...), kind=kOutput, calls=%fused_computation.11 | convolution fusion | flops 1076101120 | bytes 9963648 | tf_op jit(solution)/shard_map/dot_general | solution.py:17
  234.7 0.5 fusion.6
  235.2 0.4 copy.14
  235.6 27.6 %all_to_all.5 = bf16[16,128,3,128]{3,1,2,0:T(8,128)(2,1)S(1)} all-to-all(bf16[16,128,3,128]{3,1,2,0:T(8,128)(2,1)S(1)} %copy.14), channel_id=1, replica_groups=mesh['leaf'=8,'front'=16] {'front'}, dimensions={0} | all-to-all | bytes 3145728 | tf_op jit(solution)/shard_map/all_to_all | solution.py:96
  263.2 3.0 collective-permute-start
  266.2 33.3 %collective-permute-done = bf16[16,128,3,128]{3,1,2,0:T(8,128)(2,1)S(1)} collective-permute-done((bf16[16,128,3,128]{3,1,2,0:T(8,128)(2,1)S(1)}, bf16[16,128,3,128]{3,1,2,0:T(8,128)(2,1)S(1)}, u32[]{:S(2)}, u32[]{:S(2)}) %collective-permute-start) | collective-permute-done | bytes 1572896 | tf_op jit(solution)/shard_map/ppermute | solution.py:13
  299.5 1.4 copy.15
  300.9 2.4 reshape.114
  303.3 5.0 %fusion.24 = f32[32,49152]{1,0:T(8,128)} fusion(bf16[16,49152]{1,0:T(8,128)(2,1)} %reshape.114, s32[16]{0:T(128)S(1)} %get-tuple-element.3), kind=kOutput, calls=%fused_computation.26 | convolution fusion | flops 50332160 | bytes 7864384 | tf_op jit(solution)/shard_map/dot_general | solution.py:51
  308.3 6.1 %broadcast_in_dim_reshape.3 = f32[1,4096,384]{2,1,0:T(8,128)} reshape(f32[32,49152]{1,0:T(8,128)} %fusion.24) | data formatting | bytes 12582912 | tf_op jit(solution)/shard_map/broadcast_in_dim;reshape | solution.py:99
  (26 shorter events, 0.8 us)
Async XLA Ops:
  7.2 51.3 %all-gather.11.cloned.1.call-start = ((), (), s32[]{:S(2)}) async-start(), calls=%async_computation.3 | async-start | bytes 2228224 | tf_op jit(solution)/shard_map/all_gather | solution.py:70
  8.9 96.8 %all-gather.13.cloned.1.call-start = ((), (), s32[]{:S(2)}) async-start(), calls=%async_computation.4 | async-start | bytes 2228224 | tf_op jit(solution)/shard_map/all_gather | solution.py:76
  9.7 143.4 %all-gather.7.cloned.1.call-start = ((), (), s32[]{:S(2)}) async-start(), calls=%async_computation.1 | async-start | bytes 2228224 | tf_op jit(solution)/shard_map/all_gather | solution.py:74
  10.7 142.3 %copy-start.1 = (bf16[1,128,2048]{2,1,0:T(8,128)(2,1)S(1)}, bf16[1,128,2048]{2,1,0:T(8,128)(2,1)}, u32[]{:S(2)}) copy-start(bf16[1,128,2048]{2,1,0:T(8,128)(2,1)} %param.9) | copy-start | bytes 1572868
  61.7 166.5 %all-gather.9.cloned.1.call-start = ((), (), s32[]{:S(2)}) async-start(), calls=%async_computation.2 | async-start | bytes 8912896 | tf_op jit(solution)/shard_map/all_gather | solution.py:80
  156.8 1.2 copy-start.4
  156.8 3.3 %copy-start.2 = (s32[8,32]{1,0:T(8,128)S(1)}, s32[8,32]{1,0:T(8,128)}, u32[]{:S(2)}) copy-start(s32[8,32]{1,0:T(8,128)} %param.13) | copy-start | bytes 3076
  156.8 3.3 %copy-start.3 = (s32[8,16]{1,0:T(8,128)S(1)}, s32[8,16]{1,0:T(8,128)}, u32[]{:S(2)}) copy-start(s32[8,16]{1,0:T(8,128)} %param.12) | copy-start | bytes 1540
  156.8 71.4 %copy-start = (bf16[1,128,2048]{2,1,0:T(8,128)(2,1)S(1)}, bf16[1,128,2048]{2,1,0:T(8,128)(2,1)}, u32[]{:S(2)}) copy-start(bf16[1,128,2048]{2,1,0:T(8,128)(2,1)} %param.10) | copy-start | bytes 1572868
  263.2 36.3 %collective-permute-start = (bf16[16,128,3,128]{3,1,2,0:T(8,128)(2,1)S(1)}, bf16[16,128,3,128]{3,1,2,0:T(8,128)(2,1)S(1)}, u32[]{:S(2)}, u32[]{:S(2)}) collective-permute-start(bf16[16,128,3,128]{3,1,2,0:T(8,128)(2,1)S(1)} %all_to_all.5), channel_id=1, source_target_pairs={{0,64},{16,80},{32,96},{48,112},{64,0},{80,16},{96,32},{112,48},{1... | collective-permute-start | bytes 4718600 | tf_op jit(solution)/shard_map/ppermute | solution.py:13
Sparse Core Ops, SparseCore 0:
  10.7 47.7 all-gather.10
  61.2 44.5 all-gather.12
  108.5 44.5 all-gather.6
  158.1 70.1 all-gather.8
where the time goes:
time: 321 us
  waiting for transfers between devices  241 us (75%)
  blocking collectives  27.6 us (9%)
  matrix products  18.1 us (6%)
  local copies, waits for them, and re-layouts  14.5 us (5%)
  between operations  13.9 us (4%)
    all_gather x1, waiting for transfers between devices, per_device(): lax.all_gather(factor_local, 'front', axis=0, tiled=True)  67.8 us
    all_gather x1, waiting for transfers between devices, per_device(): lax.all_gather(first_inv, 'front', axis=0, tiled=True)  47.8 us
    all_gather x1, waiting for transfers between devices, per_device(): lax.all_gather(link_local, 'front', axis=0, tiled=True)  47.3 us
    all_gather x1, waiting for transfers between devices, per_device(): lax.all_gather(second_inv, 'front', axis=0, tiled=True)  43.9 us
    ppermute x1, waiting for transfers between devices, passed_along(): lax.ppermute(value, axis, [(i, (i + by) % devices) for i in range(devices)])  33.3 us
    all_to_all x1, blocking collectives, per_device(): lax.all_to_all(routed, 'front', split_axis=0, concat_axis=0, tiled=True)  27.6 us
    dot_general x3, matrix products, dot_rows(): lax.dot_general(left_rows, right_rows, (((1,), (1,)), ((), ())), preferre...  12.6 us
  transfers between devices with their start and end apart: 5, of which 5 were waited for; matrix products, arithmetic and copies ran while one was open for 2% of the time, Pallas kernels for 0%

commit v1 on v0

--- a/solution.py
+++ b/solution.py
@@ -6,6 +6,13 @@
 PANEL = 1024
 BLOCK = 128
 SLOTS = 3
+
+
+def gather_over(x, name, dim):
+    size = lax.axis_size(name)
+    pieces = jnp.stack([x for _ in range(size)])
+    pieces = lax.all_to_all(pieces, name, split_axis=0, concat_axis=0)
+    return jnp.concatenate(pieces, axis=dim)
 
 
 def passed_along(value, axis, by):
@@ -67,7 +74,7 @@
     right_cols = border[0, :, PANEL:]
     stacked = jnp.concatenate([upper_rows, left_cols], axis=0)
     upper_count = upper_rows.shape[0]
-    projected = against(stacked, lax.all_gather(first_inv, "front", axis=0, tiled=True))
+    projected = against(stacked, gather_over(first_inv, "front", 0))
     projected = projected.astype(jnp.bfloat16)
     link_local = projected[:upper_count]
     first_local = projected[upper_count:]

time: 321 us -> 288 us (0.90)
  waiting for transfers between devices: 241 us -> 201 us
  starting transfers between devices: 3.17 us -> 11.2 us
    all_gather x1 -> x0, waiting for transfers between devices: 47.8 us -> none  [per_device(): lax.all_gather(first_inv, 'front', axis=0, tiled=True)]
    all_to_all x0 -> x1, waiting for transfers between devices: none -> 32.3 us  [gather_over(): pieces = lax.all_to_all(pieces, name, split_axis=0, concat_axis=0)]
    all_gather x1, waiting for transfers between devices: 43.9 us -> 20.2 us  [per_device(): lax.all_gather(second_inv, 'front', axis=0, tiled=True)]
    all_to_all x0 -> x1, starting transfers between devices: none -> 8.12 us  [gather_over(): pieces = lax.all_to_all(pieces, name, split_axis=0, concat_axis=0)]
where the time goes in v1:
time: 288 us
  waiting for transfers between devices  201 us (70%)
  blocking collectives  27.6 us (10%)
  matrix products  16.4 us (6%)
  local copies, waits for them, and re-layouts  15.1 us (5%)
  between operations  13.9 us (5%)
  starting transfers between devices  11.2 us (4%)
    all_gather x1, waiting for transfers between devices, per_device(): lax.all_gather(factor_local, 'front', axis=0, tiled=True)  67.8 us
    all_gather x1, waiting for transfers between devices, per_device(): lax.all_gather(link_local, 'front', axis=0, tiled=True)  47.3 us
    ppermute x1, waiting for transfers between devices, passed_along(): lax.ppermute(value, axis, [(i, (i + by) % devices) for i in range(devices)])  33.3 us
    all_to_all x1, waiting for transfers between devices, gather_over(): pieces = lax.all_to_all(pieces, name, split_axis=0, concat_axis=0)  32.3 us
    all_to_all x1, blocking collectives, per_device(): lax.all_to_all(routed, 'front', split_axis=0, concat_axis=0, tiled=True)  27.6 us
    all_gather x1, waiting for transfers between devices, per_device(): lax.all_gather(second_inv, 'front', axis=0, tiled=True)  20.2 us
    dot_general x3, matrix products, dot_rows(): lax.dot_general(left_rows, right_rows, (((1,), (1,)), ((), ())), preferre...  10.9 us
    all_to_all x1, starting transfers between devices, gather_over(): pieces = lax.all_to_all(pieces, name, split_axis=0, concat_axis=0)  8.12 us
  transfers between devices with their start and end apart: 5, of which 5 were waited for; matrix products, arithmetic and copies ran while one was open for 2% of the time, Pallas kernels for 0%

profile of v1, /device:TPU:0, one launch (start us, length us, event | category | flops | bytes accessed | tf_op | source)
XLA Modules:
  0.0 288.0 jit_solution(10922062571506478428)
XLA Ops:
  7.2 1.6 fusion.28
  8.9 1.6 stack.3
  10.5 8.1 %all-to-all-start = ((bf16[16,64,1024]{2,1,0:T(8,128)(2,1)}), bf16[16,64,1024]{2,1,0:T(8,128)(2,1)S(1)}, u32[]{:S(2)}, u32[]{:S(2)}) async-start(bf16[16,64,1024]{2,1,0:T(8,128)(2,1)} %stack.3), calls=%async_computation | async-start | bytes 4194304 | tf_op jit(solution)/shard_map/all_to_all | solution.py:14
  18.7 32.3 %all-to-all-done = bf16[16,64,1024]{2,1,0:T(8,128)(2,1)S(1)} async-done(((bf16[16,64,1024]{2,1,0:T(8,128)(2,1)}), bf16[16,64,1024]{2,1,0:T(8,128)(2,1)S(1)}, u32[]{:S(2)}, u32[]{:S(2)}) %all-to-all-start) | async-done | bytes 2097184 | tf_op jit(solution)/shard_map/all_to_all | solution.py:14
  51.0 0.8 convolution_convert_fusion.1
  51.8 0.7 fusion.27
  52.6 20.2 %all-gather.9.cloned.1.call-done = bf16[1,1,1024,1024]{3,2,1,0:T(8,128)(2,1)} async-done(((bf16[1,1,64,1024]{3,2,1,0:T(8,128)(2,1)}), bf16[1,1,1024,1024]{3,2,1,0:T(8,128)(2,1)}) %all-gather.9.cloned.1.call-update) | async-done | bytes 2097168 | tf_op jit(solution)/shard_map/all_gather | solution.py:83
  72.8 47.3 %all-gather.5.cloned.1.call-done = bf16[1024,1024]{1,0:T(8,128)(2,1)} async-done(((bf16[64,1024]{1,0:T(8,128)(2,1)}), bf16[1024,1024]{1,0:T(8,128)(2,1)}) %all-gather.5.cloned.1.call-update) | async-done | bytes 2097168 | tf_op jit(solution)/shard_map/all_gather | solution.py:81
  120.1 3.7 %fusion.6 = bf16[128,1024]{1,0:T(8,128)(2,1)S(1)} fusion(bf16[1,1,1024,1024]{3,2,1,0:T(8,128)(2,1)} %all-gather.9.cloned.1.call-done, bf16[1024,1024]{1,0:T(8,128)(2,1)} %all-gather.5.cloned.1.call-done, bf16[1,128,2048]{2,1,0:T(8,128)(2,1)S(1)} %copy-done.1, bf16[192,1024]{1,0:T(8,128)(2,1)S(1)} %convolution_convert_fusion.1), kind=kOutput, calls=%fused_computation.10 | convolution fusion | flops 537395200 | bytes 4980736 | tf_op jit(solution)/shard_map/dot_general | solution.py:24
  123.9 1.1 pad_maximum_fusion
  125.0 0.7 dynamic_slice.3
  125.7 0.7 add_compare_fusion
  126.4 0.7 iota_compare_fusion.4
  127.5 67.8 %all-gather.7.cloned.1.call-done = bf16[2048,2048]{1,0:T(8,128)(2,1)} async-done(((bf16[128,2048]{1,0:T(8,128)(2,1)}), bf16[2048,2048]{1,0:T(8,128)(2,1)}) %all-gather.7.cloned.1.call-update) | async-done | bytes 8388624 | tf_op jit(solution)/shard_map/all_gather | solution.py:87
  195.3 6.3 %fusion.5 = bf16[16,8,16,128]{3,1,2,0:T(8,128)(2,1)S(1)} fusion(bf16[2048,2048]{1,0:T(8,128)(2,1)} %all-gather.7.cloned.1.call-done, bf16[1,128,2048]{2,1,0:T(8,128)(2,1)S(1)} %copy-done, pred[2048]{0:T(1024)(128)(4,1)S(1)} %iota_compare_fusion.4, pred[128]{0:T(512)(128)(4,1)S(1)} %add_compare_fusion, bf16[128,1024]{1,0:T(8,128)(2,1)S(1)} %fusion.6, ...), kind=kOutput, calls=%fused_computation.9 | convolution fusion | flops 1076101120 | bytes 9963648 | tf_op jit(solution)/shard_map/dot_general | solution.py:24
  201.7 0.5 fusion.4
  202.3 0.4 copy.14
  202.7 27.6 %all_to_all.10 = bf16[16,128,3,128]{3,1,2,0:T(8,128)(2,1)S(1)} all-to-all(bf16[16,128,3,128]{3,1,2,0:T(8,128)(2,1)S(1)} %copy.14), channel_id=1, replica_groups=mesh['leaf'=8,'front'=16] {'front'}, dimensions={0} | all-to-all | bytes 3145728 | tf_op jit(solution)/shard_map/all_to_all | solution.py:103
  230.3 3.0 %collective-permute-start = (bf16[16,128,3,128]{3,1,2,0:T(8,128)(2,1)S(1)}, bf16[16,128,3,128]{3,1,2,0:T(8,128)(2,1)S(1)}, u32[]{:S(2)}, u32[]{:S(2)}) collective-permute-start(bf16[16,128,3,128]{3,1,2,0:T(8,128)(2,1)S(1)} %all_to_all.10), channel_id=1, source_target_pairs={{0,64},{16,80},{32,96},{48,112},{64,0},{80,16},{96,32},{112,48},{1... | collective-permute-start | bytes 4718600 | tf_op jit(solution)/shard_map/ppermute | solution.py:20
  233.3 33.3 %collective-permute-done = bf16[16,128,3,128]{3,1,2,0:T(8,128)(2,1)S(1)} collective-permute-done((bf16[16,128,3,128]{3,1,2,0:T(8,128)(2,1)S(1)}, bf16[16,128,3,128]{3,1,2,0:T(8,128)(2,1)S(1)}, u32[]{:S(2)}, u32[]{:S(2)}) %collective-permute-start) | collective-permute-done | bytes 1572896 | tf_op jit(solution)/shard_map/ppermute | solution.py:20
  266.6 1.4 copy.15
  268.0 2.4 reshape.120
  270.3 5.0 %fusion.19 = f32[32,49152]{1,0:T(8,128)} fusion(bf16[16,49152]{1,0:T(8,128)(2,1)} %reshape.120, s32[16]{0:T(128)S(1)} %get-tuple-element.3), kind=kOutput, calls=%fused_computation.25 | convolution fusion | flops 50332160 | bytes 7864384 | tf_op jit(solution)/shard_map/dot_general | solution.py:58
  275.3 6.1 %broadcast_in_dim_reshape.3 = f32[1,4096,384]{2,1,0:T(8,128)} reshape(f32[32,49152]{1,0:T(8,128)} %fusion.19) | data formatting | bytes 12582912 | tf_op jit(solution)/shard_map/broadcast_in_dim;reshape | solution.py:106
  (28 shorter events, 0.7 us)
Async XLA Ops:
  7.2 65.7 %all-gather.9.cloned.1.call-start = ((), (), s32[]{:S(2)}) async-start(), calls=%async_computation.4 | async-start | bytes 2228224 | tf_op jit(solution)/shard_map/all_gather | solution.py:83
  10.5 8.2 %copy-start.1 = (bf16[1,128,2048]{2,1,0:T(8,128)(2,1)S(1)}, bf16[1,128,2048]{2,1,0:T(8,128)(2,1)}, u32[]{:S(2)}) copy-start(bf16[1,128,2048]{2,1,0:T(8,128)(2,1)} %param.9) | copy-start | bytes 1572868
  10.5 40.5 %copy-start.4 = (bf16[1,64,1024]{2,1,0:T(8,128)(2,1)S(1)}, bf16[1,64,1024]{2,1,0:T(8,128)(2,1)}, u32[]{:S(2)}) copy-start(bf16[1,64,1024]{2,1,0:T(8,128)(2,1)} %param.8) | copy-start | bytes 393220
  10.5 40.5 %all-to-all-start = ((bf16[16,64,1024]{2,1,0:T(8,128)(2,1)}), bf16[16,64,1024]{2,1,0:T(8,128)(2,1)S(1)}, u32[]{:S(2)}, u32[]{:S(2)}) async-start(bf16[16,64,1024]{2,1,0:T(8,128)(2,1)} %stack.3), calls=%async_computation | async-start | bytes 4194304 | tf_op jit(solution)/shard_map/all_to_all | solution.py:14
  18.6 101.5 %all-gather.5.cloned.1.call-start = ((), (), s32[]{:S(2)}) async-start(), calls=%async_computation.2 | async-start | bytes 2228224 | tf_op jit(solution)/shard_map/all_gather | solution.py:81
  52.6 142.7 %all-gather.7.cloned.1.call-start = ((), (), s32[]{:S(2)}) async-start(), calls=%async_computation.3 | async-start | bytes 8912896 | tf_op jit(solution)/shard_map/all_gather | solution.py:87
  123.8 1.2 copy-start.5
  123.9 3.3 %copy-start.2 = (s32[8,32]{1,0:T(8,128)S(1)}, s32[8,32]{1,0:T(8,128)}, u32[]{:S(2)}) copy-start(s32[8,32]{1,0:T(8,128)} %param.13) | copy-start | bytes 3076
  123.9 3.3 %copy-start.3 = (s32[8,16]{1,0:T(8,128)S(1)}, s32[8,16]{1,0:T(8,128)}, u32[]{:S(2)}) copy-start(s32[8,16]{1,0:T(8,128)} %param.12) | copy-start | bytes 1540
  123.9 71.4 %copy-start = (bf16[1,128,2048]{2,1,0:T(8,128)(2,1)S(1)}, bf16[1,128,2048]{2,1,0:T(8,128)(2,1)}, u32[]{:S(2)}) copy-start(bf16[1,128,2048]{2,1,0:T(8,128)(2,1)} %param.10) | copy-start | bytes 1572868
  230.3 36.3 %collective-permute-start = (bf16[16,128,3,128]{3,1,2,0:T(8,128)(2,1)S(1)}, bf16[16,128,3,128]{3,1,2,0:T(8,128)(2,1)S(1)}, u32[]{:S(2)}, u32[]{:S(2)}) collective-permute-start(bf16[16,128,3,128]{3,1,2,0:T(8,128)(2,1)S(1)} %all_to_all.10), channel_id=1, source_target_pairs={{0,64},{16,80},{32,96},{48,112},{64,0},{80,16},{96,32},{112,48},{1... | collective-permute-start | bytes 4718600 | tf_op jit(solution)/shard_map/ppermute | solution.py:20
Sparse Core Ops, SparseCore 0:
  10.7 62.0 all-gather.8
  75.5 44.5 all-gather.4
  125.1 70.1 all-gather.6
